TPU v7x, 512 devices: a whole 4x8x8 slice. The times are simulated.
512 devices in a mesh: dp: 16 (over x, z_lo, core), ctx: 32 (over z_hi, y).
Axes of the slice: x: 4, y: 8, z: 8 (z_hi: 4, z_lo: 2; z = z_hi * 2 + z_lo), core: 2. Of those that a mesh axis runs over, the one named last changes fastest.
Arguments:
- queries: bfloat16 [16, 4096, 1024], P('dp', 'ctx'), may hold values from -60 to 60
- keys: bfloat16 [16, 4096, 128], P('dp', 'ctx'), may hold values from -6 to 6
- values: bfloat16 [16, 4096, 192], P('dp', 'ctx'), may hold values from -96 to 96
- features_fine: bfloat16 [16, 8192, 1536], P('dp', 'ctx'), may hold values from -6 to 6
- rc_state: bfloat16 [16, 4096, 1536], P('dp', 'ctx'), may hold values from -6 to 6
- conv_weight: float32 [5, 1536], replicated, may hold values from -2.5 to 2.5
Outputs:
- d_fine: bfloat16 [16, 8192, 1536], P('dp', 'ctx')
- d_weight: float32 [5, 1536], replicated
All inputs are finite; a program needn't handle non-finite values.
Results may differ from a plain program's by a relative error of at most 0.0085.
Values may be sent and summed in bfloat16 or wider, within the bound.
A program may use at most 64 MiB of HBM per device.

v0:
```python
import math
import jax
import jax.numpy as jnp
from jax import lax
from jax.sharding import PartitionSpec as P

HEADS = 8
KW = 5


def padded_2(cells, sides, width):
    for axis, dim in sides:
        count = lax.axis_size(axis)
        ends = count - 1
        head = lax.slice_in_dim(cells, 0, width, axis=dim)
        tail = lax.slice_in_dim(cells, cells.shape[dim] - width, cells.shape[dim], axis=dim)
        cells = jnp.concatenate(
            [
                lax.ppermute(tail, axis, [(i, (i + 1) % count) for i in range(ends)]),
                cells,
                lax.ppermute(head, axis, [((i + 1) % count, i) for i in range(ends)]),
            ],
            axis=dim,
        )
    return cells


def body(queries, keys, values, features_fine, rc_state, conv_weight):
    tok_rows = queries.shape[1]
    key_size = keys.shape[2]
    value_size = values.shape[2]
    q_heads = queries[0].reshape(tok_rows, HEADS, key_size)
    ctx_count = lax.axis_size("ctx")
    run_top = jnp.full((tok_rows, HEADS), -1e30, jnp.float32)
    key_piece = lax.all_gather(keys, "ctx", axis=1, tiled=True)
    value_piece = lax.all_gather(values, "ctx", axis=1, tiled=True)
    scores = jnp.einsum(
        "qhd,kd->qhk", q_heads, key_piece[0], preferred_element_type=jnp.float32
    ) * key_size ** (-0.5)
    new_top = jnp.maximum(run_top, jnp.max(scores, axis=-1))
    expd = jnp.exp(scores - new_top[..., None])
    new_total = jnp.sum(expd, axis=-1)
    mixed = jnp.einsum(
        "qhk,kv->qhv", expd.astype(jnp.bfloat16), value_piece[0], preferred_element_type=jnp.float32
    )
    attended = (mixed / new_total[..., None]).reshape(tok_rows, HEADS * value_size)[None]
    padded = padded_2(features_fine, (("ctx", 1),), 2)
    taps = [padded[:, k : k + 2 * tok_rows : 2, :].astype(jnp.float32) for k in range(KW)]
    coarse = conv_weight[0] * taps[0]
    for k in range(1, KW):
        coarse = coarse + conv_weight[k] * taps[k]
    slices = lax.all_to_all(rc_state, "ctx", split_axis=2, concat_axis=0, tiled=True)
    flipped = slices[::-1]
    mirrored = lax.all_to_all(flipped, "ctx", split_axis=0, concat_axis=2, tiled=True)
    grad = coarse + attended - mirrored[:, ::-1, :].astype(jnp.float32)
    gpad = padded_2(grad.astype(jnp.bfloat16), (("ctx", 1),), 1).astype(grad.dtype)
    even = (
        conv_weight[0] * gpad[:, 2:]
        + conv_weight[2] * gpad[:, 1:-1]
        + conv_weight[4] * gpad[:, :-2]
    )
    odd = conv_weight[1] * gpad[:, 2:] + conv_weight[3] * gpad[:, 1:-1]
    d_fine = (
        jnp.stack([even, odd], axis=2)
        .reshape(grad.shape[0], 2 * tok_rows, grad.shape[2])
        .astype(jnp.bfloat16)
    )
    partial_grad = jnp.stack([jnp.sum(grad * taps[k], axis=(0, 1)) for k in range(KW)])
    summed = lax.psum(partial_grad, ("dp", "ctx"))
    scale = 1.0 / math.sqrt(lax.axis_size("dp") * tok_rows * ctx_count)
    return (d_fine, summed * scale)


def solution(mesh):
    placed = (
        P("dp", "ctx", None),
        P("dp", "ctx", None),
        P("dp", "ctx", None),
        P("dp", "ctx", None),
        P("dp", "ctx", None),
        P(),
    )
    return jax.shard_map(
        body, mesh=mesh, in_specs=placed, out_specs=(P("dp", "ctx", None), P()), check_vma=False
    )
```

profile of v0, /device:TPU:184, one launch (start us, length us, event | category | flops | bytes accessed | tf_op | source)
XLA Modules:
  0.0 341.5 jit_solution(18383458230890813925)
XLA Ops:
  7.2 0.0 all-gather.3.cloned.1.call-start
  7.2 0.7 all-gather.3.cloned.1.call-update
  7.9 2.2 copy.29
  10.1 0.5 broadcast.15
  10.6 8.8 %reduce.10 = bf16[1536,128]{1,0:T(8,128)(2,1)S(1)} reduce(bf16[1536,1,128]{2,1,0:T(2,128)(2,1)S(1)} %bitcast.34, bf16[]{:T(256)} %broadcast.15), dimensions={1}, to_apply=%bitcast.29.reduce_sub_computation | reduce | bytes 786434
  19.4 0.8 reshape.84
  20.2 13.8 %all-to-all-start = ((bf16[32,2,3072]{2,1,0:T(2,128)(2,1)}), bf16[32,2,3072]{2,1,0:T(2,128)(2,1)S(1)}, u32[]{:S(2)}, u32[]{:S(2)}) async-start(bf16[32,2,3072]{2,1,0:T(2,128)(2,1)} %reshape.84), calls=%async_computation | async-start | bytes 786432 | tf_op jit(solution)/shard_map/all_to_all | solution.py:52
  34.0 0.0 all-gather.5.cloned.1.call-start
  34.1 0.7 all-gather.5.cloned.1.call-update
  34.8 12.8 %all-to-all-done = bf16[32,2,3072]{2,1,0:T(2,128)(2,1)S(1)} async-done(((bf16[32,2,3072]{2,1,0:T(2,128)(2,1)}), bf16[32,2,3072]{2,1,0:T(2,128)(2,1)S(1)}, u32[]{:S(2)}, u32[]{:S(2)}) %all-to-all-start) | async-done | bytes 393248 | tf_op jit(solution)/shard_map/all_to_all | solution.py:52
  47.6 0.3 reshape.85
  47.9 0.1 copy.31
  48.0 0.8 rev.6
  48.7 8.5 %all-to-all-start.1 = ((bf16[32,128,48]{1,2,0:T(8,128)(2,1)}), bf16[32,128,48]{1,2,0:T(8,128)(2,1)S(1)}, u32[]{:S(2)}, u32[]{:S(2)}) async-start(bf16[32,128,48]{1,2,0:T(8,128)(2,1)} %rev.6), calls=%async_computation.1 | async-start | bytes 786432 | tf_op jit(solution)/shard_map/all_to_all | solution.py:54
  57.3 0.3 copy.24
  57.5 5.5 %collective-permute-start = (bf16[1,2,1536]{1,2,0:T(8,128)(2,1)S(1)}, bf16[1,2,1536]{1,2,0:T(8,128)(2,1)}, u32[]{:S(2)}, u32[]{:S(2)}) collective-permute-start(bf16[1,2,1536]{1,2,0:T(8,128)(2,1)S(1)} %copy.24), channel_id=1, source_target_pairs={{0,1},{1,2},{2,3},{3,4},{4,5},{5,6},{6,7},{7,8},{8,9},{9,10},{10,1... | collective-permute-start | bytes 18440 | tf_op jit(solution)/shard_map/ppermute | solution.py:19
  63.0 0.3 copy.25
  63.3 2.1 collective-permute-start.1
  65.4 0.1 slice_reduce_fusion.4
  65.5 0.3 copy.26
  65.8 1.0 copy.32
  66.8 14.4 %slice.65 = bf16[1,128,1536]{1,2,0:T(8,128)(2,1)S(1)} slice(bf16[1,256,1536]{1,2,0:T(8,128)(2,1)S(1)} %copy.26), slice={[0:1:1], [0:256:2], [0:1536:1]} | slice | bytes 786432 | tf_op jit(solution)/shard_map/slice | solution.py:48
  81.2 5.9 %collective-permute-done.1 = bf16[1,2,1536]{1,2,0:T(8,128)(2,1)} collective-permute-done((bf16[1,2,1536]{1,2,0:T(8,128)(2,1)S(1)}, bf16[1,2,1536]{1,2,0:T(8,128)(2,1)}, u32[]{:S(2)}, u32[]{:S(2)}) %collective-permute-start.1) | collective-permute-done | bytes 6176 | tf_op jit(solution)/shard_map/ppermute | solution.py:21
  87.1 1.8 pad_maximum_fusion
  88.9 14.4 %slice.61 = bf16[1,128,1536]{1,2,0:T(8,128)(2,1)S(1)} slice(bf16[1,260,1536]{1,2,0:T(8,128)(2,1)S(1)} %pad_maximum_fusion), slice={[0:1:1], [0:256:2], [0:1536:1]} | slice | bytes 786432 | tf_op jit(solution)/shard_map/slice | solution.py:48
  103.3 14.4 %slice.63 = bf16[1,128,1536]{1,2,0:T(8,128)(2,1)S(1)} slice(bf16[1,260,1536]{1,2,0:T(8,128)(2,1)S(1)} %pad_maximum_fusion), slice={[0:1:1], [1:257:2], [0:1536:1]} | slice | bytes 786432 | tf_op jit(solution)/shard_map/slice | solution.py:48
  117.7 14.7 %slice.67 = bf16[1,128,1536]{1,2,0:T(8,128)(2,1)S(1)} slice(bf16[1,260,1536]{1,2,0:T(8,128)(2,1)S(1)} %pad_maximum_fusion), slice={[0:1:1], [3:259:2], [0:1536:1]} | slice | bytes 786432 | tf_op jit(solution)/shard_map/slice | solution.py:48
  132.4 15.0 %slice.69 = bf16[1,128,1536]{1,2,0:T(8,128)(2,1)} slice(bf16[1,260,1536]{1,2,0:T(8,128)(2,1)S(1)} %pad_maximum_fusion), slice={[0:1:1], [4:260:2], [0:1536:1]} | slice | bytes 786432 | tf_op jit(solution)/shard_map/slice | solution.py:48
  147.4 1.3 rev.7
  148.7 0.0 all-gather.3.cloned.1.call-done
  148.8 9.3 %multiply_reduce_fusion = (f32[128,8]{0,1:T(8,128)S(1)}, f32[128,8,4096]{2,0,1:T(8,128)}) fusion(bf16[1,4096,128]{2,1,0:T(8,128)(2,1)} %all-gather.3.cloned.1.call-done, bf16[128,8,128]{2,1,0:T(8,128)(2,1)S(1)} %bitcast.36), kind=kOutput, calls=%fused_computation.1 | convolution fusion | flops 1082129408 | bytes 18092032 | tf_op jit(solution)/shard_map/qhd,kd->qhk/dot_general | solution.py:37
  158.0 8.6 %fusion = f32[128,8]{0,1:T(8,128)S(1)} fusion(f32[128,8,4096]{2,0,1:T(8,128)} %get-tuple-element.20, f32[128,8]{0,1:T(8,128)S(1)} %broadcast_maximum_fusion), kind=kLoop, calls=%fused_computation.2 | loop fusion | flops 12581888 | bytes 16785408 | tf_op jit(solution)/shard_map/reduce_sum | solution.py:42
  166.7 29.0 %all-gather.5.cloned.1.call-done = bf16[1,4096,192]{1,2,0:T(8,128)(2,1)} async-done(((bf16[1,128,192]{1,2,0:T(8,128)(2,1)}), bf16[1,4096,192]{1,2,0:T(8,128)(2,1)}) %all-gather.5.cloned.1.call-update) | async-done | bytes 1572880 | tf_op jit(solution)/shard_map/all_gather | solution.py:36
  195.6 8.0 %fusion.7 = f32[128,8,192]{0,2,1:T(8,128)S(1)} fusion(bf16[1,4096,192]{1,2,0:T(8,128)(2,1)} %all-gather.5.cloned.1.call-done, f32[128,8,4096]{2,0,1:T(8,128)} %get-tuple-element.20, f32[128,8]{0,1:T(8,128)S(1)} %broadcast_maximum_fusion, f32[128,8]{0,1:T(8,128)S(1)} %fusion), kind=kOutput, calls=%fused_computation.19 | convolution fusion | flops 1623392256 | bytes 19144704 | tf_op jit(solution)/shard_map/qhk,kv->qhv/dot_general | solution.py:43
  203.6 2.7 fusion.22
  206.4 0.1 stack.38
  206.5 93.2 %psum.7 = f32[5,1536]{1,0:T(8,128)S(1)} all-reduce(f32[5,1536]{1,0:T(8,128)S(1)} %stack.38), channel_id=1, replica_groups=mesh['dp'=16,'ctx'=32] {'dp','ctx'}, use_global_device_ids=true, to_apply=%region_7.0 | all-reduce | flops 7680 | bytes 61440 | tf_op jit(solution)/shard_map/psum | solution.py:69
  299.7 0.2 fusion.31
  299.9 6.2 %collective-permute-start.2 = (bf16[1,1,1536]{1,2,0:T(8,128)(2,1)S(1)}, bf16[1,1,1536]{1,2,0:T(8,128)(2,1)S(1)}, u32[]{:S(2)}, u32[]{:S(2)}) collective-permute-start(bf16[1,1,1536]{1,2,0:T(8,128)(2,1)S(1)} %get-tuple-element.17), channel_id=1, source_target_pairs={{0,1},{1,2},{2,3},{3,4},{4,5},{5,6},{6,7},{7,8},{8,9},{9,10},{10,1... | collective-permute-start | bytes 9224 | tf_op jit(solution)/shard_map/ppermute | solution.py:19
  306.1 1.9 collective-permute-start.3
  308.0 0.6 broadcast_multiply_fusion
  308.6 11.6 %collective-permute-done.2 = bf16[1,1,1536]{1,2,0:T(8,128)(2,1)S(1)} collective-permute-done((bf16[1,1,1536]{1,2,0:T(8,128)(2,1)S(1)}, bf16[1,1,1536]{1,2,0:T(8,128)(2,1)S(1)}, u32[]{:S(2)}, u32[]{:S(2)}) %collective-permute-start.2) | collective-permute-done | bytes 3104 | tf_op jit(solution)/shard_map/ppermute | solution.py:19
  320.2 10.3 %collective-permute-done.3 = bf16[1,1,1536]{1,2,0:T(8,128)(2,1)S(1)} collective-permute-done((bf16[1,1,1536]{1,2,0:T(8,128)(2,1)S(1)}, bf16[1,1,1536]{1,2,0:T(8,128)(2,1)S(1)}, u32[]{:S(2)}, u32[]{:S(2)}) %collective-permute-start.3) | collective-permute-done | bytes 3104 | tf_op jit(solution)/shard_map/ppermute | solution.py:21
  330.5 0.4 maximum_convert_fusion
  330.9 1.7 fusion.26
  332.6 0.1 pad_maximum_fusion.1
  332.7 0.8 copy.30
  333.5 1.2 convert_element_type.56
  (15 shorter events, 0.1 us)
Async XLA Ops:
  7.2 141.6 %all-gather.3.cloned.1.call-start = ((), (), s32[]{:S(2)}) async-start(), calls=%async_computation.2 | async-start | bytes 1081344 | tf_op jit(solution)/shard_map/all_gather | solution.py:35
  20.2 37.0 %copy-start.1 = (bf16[1,256,1536]{2,1,0:T(8,128)(2,1)S(1)}, bf16[1,256,1536]{2,1,0:T(8,128)(2,1)}, u32[]{:S(2)}) copy-start(bf16[1,256,1536]{2,1,0:T(8,128)(2,1)} %param.9) | copy-start | bytes 2359300
  20.2 27.4 %all-to-all-start = ((bf16[32,2,3072]{2,1,0:T(2,128)(2,1)}), bf16[32,2,3072]{2,1,0:T(2,128)(2,1)S(1)}, u32[]{:S(2)}, u32[]{:S(2)}) async-start(bf16[32,2,3072]{2,1,0:T(2,128)(2,1)} %reshape.84), calls=%async_computation | async-start | bytes 786432 | tf_op jit(solution)/shard_map/all_to_all | solution.py:52
  34.0 161.6 %all-gather.5.cloned.1.call-start = ((), (), s32[]{:S(2)}) async-start(), calls=%async_computation.3 | async-start | bytes 1622016 | tf_op jit(solution)/shard_map/all_gather | solution.py:36
  34.8 30.6 %copy-start.2 = (f32[5,1536]{1,0:T(8,128)S(1)}, f32[5,1536]{1,0:T(8,128)}, u32[]{:S(2)}) copy-start(f32[5,1536]{1,0:T(8,128)} %param.11) | copy-start | bytes 92164
  48.7 98.6 %all-to-all-start.1 = ((bf16[32,128,48]{1,2,0:T(8,128)(2,1)}), bf16[32,128,48]{1,2,0:T(8,128)(2,1)S(1)}, u32[]{:S(2)}, u32[]{:S(2)}) async-start(bf16[32,128,48]{1,2,0:T(8,128)(2,1)} %rev.6), calls=%async_computation.1 | async-start | bytes 786432 | tf_op jit(solution)/shard_map/all_to_all | solution.py:54
  57.5 23.6 %collective-permute-start = (bf16[1,2,1536]{1,2,0:T(8,128)(2,1)S(1)}, bf16[1,2,1536]{1,2,0:T(8,128)(2,1)}, u32[]{:S(2)}, u32[]{:S(2)}) collective-permute-start(bf16[1,2,1536]{1,2,0:T(8,128)(2,1)S(1)} %copy.24), channel_id=1, source_target_pairs={{0,1},{1,2},{2,3},{3,4},{4,5},{5,6},{6,7},{7,8},{8,9},{9,10},{10,1... | collective-permute-start | bytes 18440 | tf_op jit(solution)/shard_map/ppermute | solution.py:19
  63.3 23.8 %collective-permute-start.1 = (bf16[1,2,1536]{1,2,0:T(8,128)(2,1)S(1)}, bf16[1,2,1536]{1,2,0:T(8,128)(2,1)}, u32[]{:S(2)}, u32[]{:S(2)}) collective-permute-start(bf16[1,2,1536]{1,2,0:T(8,128)(2,1)S(1)} %copy.25), channel_id=1, source_target_pairs={{1,0},{2,1},{3,2},{4,3},{5,4},{6,5},{7,6},{8,7},{9,8},{10,9},{11,1... | collective-permute-start | bytes 18440 | tf_op jit(solution)/shard_map/ppermute | solution.py:21
  166.7 36.9 %copy-start = (bf16[1,128,1536]{1,2,0:T(8,128)(2,1)S(1)}, bf16[1,128,1536]{1,2,0:T(8,128)(2,1)}, u32[]{:S(2)}) copy-start(bf16[1,128,1536]{1,2,0:T(8,128)(2,1)} %slice.69) | copy-start | bytes 1179652
  299.9 20.3 %collective-permute-start.2 = (bf16[1,1,1536]{1,2,0:T(8,128)(2,1)S(1)}, bf16[1,1,1536]{1,2,0:T(8,128)(2,1)S(1)}, u32[]{:S(2)}, u32[]{:S(2)}) collective-permute-start(bf16[1,1,1536]{1,2,0:T(8,128)(2,1)S(1)} %get-tuple-element.17), channel_id=1, source_target_pairs={{0,1},{1,2},{2,3},{3,4},{4,5},{5,6},{6,7},{7,8},{8,9},{9,10},{10,1... | collective-permute-start | bytes 9224 | tf_op jit(solution)/shard_map/ppermute | solution.py:19
  306.1 24.4 %collective-permute-start.3 = (bf16[1,1,1536]{1,2,0:T(8,128)(2,1)S(1)}, bf16[1,1,1536]{1,2,0:T(8,128)(2,1)S(1)}, u32[]{:S(2)}, u32[]{:S(2)}) collective-permute-start(bf16[1,1,1536]{1,2,0:T(8,128)(2,1)S(1)} %get-tuple-element.18), channel_id=1, source_target_pairs={{1,0},{2,1},{3,2},{4,3},{5,4},{6,5},{7,6},{8,7},{9,8},{10,9},{11,1... | collective-permute-start | bytes 9224 | tf_op jit(solution)/shard_map/ppermute | solution.py:21
Sparse Core Ops, SparseCore 0:
  11.2 102.2 all-gather.2
  116.5 79.0 all-gather.4
where the time goes:
time: 342 us; the launch traced here: 341 us
  blocking collectives  93.2 us (27%)
  local copies, waits for them, and re-layouts  82.9 us (24%)
  waiting for transfers between devices  70.9 us (21%)
  starting transfers between devices  38.1 us (11%)
  other arithmetic  24.9 us (7%)
  matrix products  17.2 us (5%)
  between operations  14.3 us (4%)
    psum x1, blocking collectives, body(): summed = lax.psum(partial_grad, ('dp', 'ctx'))  93.2 us
    slice x5, local copies, waits for them, and re-layouts, body(): padded[:, k:k + 2 * tok_rows:2, :].astype(jnp.float32)  72.8 us
    all_gather x1, waiting for transfers between devices, body(): value_piece = lax.all_gather(values, 'ctx', axis=1, tiled=True)  29 us
    ppermute x2, waiting for transfers between devices, padded_2(): lax.ppermute(head, axis, [((i + 1) % count, i) for i in range(ends)])  16.2 us
    all_to_all x1, starting transfers between devices, body(): lax.all_to_all(rc_state, 'ctx', split_axis=2, concat_axis=0, tiled=True)  13.8 us
    all_to_all x1, waiting for transfers between devices, body(): lax.all_to_all(rc_state, 'ctx', split_axis=2, concat_axis=0, tiled=True)  12.8 us
    ppermute x2, starting transfers between devices, padded_2(): lax.ppermute(tail, axis, [(i, (i + 1) % count) for i in range(ends)])  11.7 us
    ppermute x2, waiting for transfers between devices, padded_2(): lax.ppermute(tail, axis, [(i, (i + 1) % count) for i in range(ends)])  11.6 us
  transfers between devices with their start and end apart: 8, of which 5 were waited for; matrix products, arithmetic and copies ran while one was open for 32% of the time, Pallas kernels for 0%

commit v1 on v0

--- a/solution.py
+++ b/solution.py
@@ -49,7 +49,10 @@
     coarse = conv_weight[0] * taps[0]
     for k in range(1, KW):
         coarse = coarse + conv_weight[k] * taps[k]
-    slices = lax.all_to_all(rc_state, "ctx", split_axis=2, concat_axis=0, tiled=True)
+    slices = jnp.concatenate(
+        lax.all_to_all(jnp.stack(jnp.split(rc_state, lax.axis_size("ctx"), axis=2)), "ctx", 0, 0),
+        axis=0,
+    )
     flipped = slices[::-1]
     mirrored = lax.all_to_all(flipped, "ctx", split_axis=0, concat_axis=2, tiled=True)
     grad = coarse + attended - mirrored[:, ::-1, :].astype(jnp.float32)

time: 342 us -> 354 us (1.035)
  local copies, waits for them, and re-layouts: 82.9 us -> 103 us
  other arithmetic: 24.9 us -> 16.1 us
    unnamed x13 -> x73, local copies, waits for them, and re-layouts: 5.16 us -> 22 us
    unnamed x1 -> x0, other arithmetic: 8.8 us -> none
  transfers between devices with their start and end apart: 8 -> 8, of which waited for: 5 -> 5; matrix products, arithmetic and copies ran while one was open for 32% -> 34% of each run, Pallas kernels for 0% -> 0%
where the time goes in v1:
time: 354 us; the launch traced here: 353 us
  local copies, waits for them, and re-layouts  103 us (29%)
  blocking collectives  93.2 us (26%)
  waiting for transfers between devices  71.3 us (20%)
  starting transfers between devices  38 us (11%)
  matrix products  17.2 us (5%)
  other arithmetic  16.1 us (5%)
  between operations  14.4 us (4%)
    psum x1, blocking collectives, body(): summed = lax.psum(partial_grad, ('dp', 'ctx'))  93.2 us
    slice x5, local copies, waits for them, and re-layouts, body(): padded[:, k:k + 2 * tok_rows:2, :].astype(jnp.float32)  72.8 us
    all_gather x1, waiting for transfers between devices, body(): value_piece = lax.all_gather(values, 'ctx', axis=1, tiled=True)  28.2 us
    unnamed x73, local copies, waits for them, and re-layouts  22 us
    ppermute x2, waiting for transfers between devices, padded_2(): lax.ppermute(head, axis, [((i + 1) % count, i) for i in range(ends)])  17.4 us
    all_to_all x1, starting transfers between devices, body(): lax.all_to_all(jnp.stack(jnp.split(rc_state, lax.axis_size('ctx'), axis=2...  13.8 us
    all_to_all x1, waiting for transfers between devices, body(): lax.all_to_all(jnp.stack(jnp.split(rc_state, lax.axis_size('ctx'), axis=2...  12.7 us
    ppermute x2, starting transfers between devices, padded_2(): lax.ppermute(tail, axis, [(i, (i + 1) % count) for i in range(ends)])  11.7 us
  transfers between devices with their start and end apart: 8, of which 5 were waited for; matrix products, arithmetic and copies ran while one was open for 34% of the time, Pallas kernels for 0%

profile of v1, /device:TPU:184, one launch (start us, length us, event | category | flops | bytes accessed | tf_op | source)
XLA Modules:
  0.0 353.5 jit_solution(1659261509632477971)
XLA Ops:
  7.2 0.7 all-gather.3.cloned.1.call-update
  7.9 1.4 fusion.33
  9.3 1.5 fusion.32
  10.9 0.6 constant_dynamic-update-slice_fusion.31
  13.8 0.6 constant_dynamic-update-slice_fusion.30
  14.4 0.6 constant_dynamic-update-slice_fusion.29
  15.0 0.6 constant_dynamic-update-slice_fusion.28
  15.6 0.6 constant_dynamic-update-slice_fusion.27
  16.2 0.6 constant_dynamic-update-slice_fusion.26
  16.8 0.6 constant_dynamic-update-slice_fusion.25
  17.4 0.6 constant_dynamic-update-slice_fusion.24
  18.0 0.6 constant_dynamic-update-slice_fusion.23
  19.9 0.6 constant_dynamic-update-slice_fusion.20
  21.7 0.6 constant_dynamic-update-slice_fusion.17
  23.5 0.6 constant_dynamic-update-slice_fusion.14
  24.7 0.6 constant_dynamic-update-slice_fusion.12
  26.5 0.6 constant_dynamic-update-slice_fusion.9
  28.9 0.6 constant_dynamic-update-slice_fusion.6
  30.1 0.6 constant_dynamic-update-slice_fusion.4
  33.2 13.8 %all-to-all-start = ((bf16[32,1,128,48]{2,3,1,0:T(8,128)(2,1)}), bf16[32,1,128,48]{2,3,1,0:T(8,128)(2,1)S(1)}, u32[]{:S(2)}, u32[]{:S(2)}) async-start(bf16[32,1,128,48]{2,3,1,0:T(8,128)(2,1)} %constant_dynamic-update-slice_fusion), calls=%async_computation | async-start | bytes 786432 | tf_op jit(solution)/shard_map/all_to_all | solution.py:53
  47.0 0.7 all-gather.5.cloned.1.call-update
  47.7 12.7 %all-to-all-done = bf16[32,1,128,48]{2,3,1,0:T(8,128)(2,1)S(1)} async-done(((bf16[32,1,128,48]{2,3,1,0:T(8,128)(2,1)}), bf16[32,1,128,48]{2,3,1,0:T(8,128)(2,1)S(1)}, u32[]{:S(2)}, u32[]{:S(2)}) %all-to-all-start) | async-done | bytes 393248 | tf_op jit(solution)/shard_map/all_to_all | solution.py:53
  60.4 0.8 rev.6
  61.2 8.4 %all-to-all-start.1 = ((bf16[32,128,48]{1,2,0:T(8,128)(2,1)}), bf16[32,128,48]{1,2,0:T(8,128)(2,1)S(1)}, u32[]{:S(2)}, u32[]{:S(2)}) async-start(bf16[32,128,48]{1,2,0:T(8,128)(2,1)} %rev.6), calls=%async_computation.1 | async-start | bytes 786432 | tf_op jit(solution)/shard_map/all_to_all | solution.py:57
  69.9 5.5 %collective-permute-start = (bf16[1,2,1536]{1,2,0:T(8,128)(2,1)S(1)}, bf16[1,2,1536]{1,2,0:T(8,128)(2,1)}, u32[]{:S(2)}, u32[]{:S(2)}) collective-permute-start(bf16[1,2,1536]{1,2,0:T(8,128)(2,1)S(1)} %copy.86), channel_id=1, source_target_pairs={{0,1},{1,2},{2,3},{3,4},{4,5},{5,6},{6,7},{7,8},{8,9},{9,10},{10,1... | collective-permute-start | bytes 18440 | tf_op jit(solution)/shard_map/ppermute | solution.py:19
  75.6 2.1 collective-permute-start.1
  78.2 14.4 %slice.65 = bf16[1,128,1536]{1,2,0:T(8,128)(2,1)S(1)} slice(bf16[1,256,1536]{1,2,0:T(8,128)(2,1)S(1)} %copy.88), slice={[0:1:1], [0:256:2], [0:1536:1]} | slice | bytes 786432 | tf_op jit(solution)/shard_map/slice | solution.py:48
  92.6 7.1 %collective-permute-done.1 = bf16[1,2,1536]{1,2,0:T(8,128)(2,1)} collective-permute-done((bf16[1,2,1536]{1,2,0:T(8,128)(2,1)S(1)}, bf16[1,2,1536]{1,2,0:T(8,128)(2,1)}, u32[]{:S(2)}, u32[]{:S(2)}) %collective-permute-start.1) | collective-permute-done | bytes 6176 | tf_op jit(solution)/shard_map/ppermute | solution.py:21
  99.7 1.8 pad_maximum_fusion
  101.6 14.4 %slice.61 = bf16[1,128,1536]{1,2,0:T(8,128)(2,1)S(1)} slice(bf16[1,260,1536]{1,2,0:T(8,128)(2,1)S(1)} %pad_maximum_fusion), slice={[0:1:1], [0:256:2], [0:1536:1]} | slice | bytes 786432 | tf_op jit(solution)/shard_map/slice | solution.py:48
  116.0 14.4 %slice.63 = bf16[1,128,1536]{1,2,0:T(8,128)(2,1)S(1)} slice(bf16[1,260,1536]{1,2,0:T(8,128)(2,1)S(1)} %pad_maximum_fusion), slice={[0:1:1], [1:257:2], [0:1536:1]} | slice | bytes 786432 | tf_op jit(solution)/shard_map/slice | solution.py:48
  130.4 14.7 %slice.67 = bf16[1,128,1536]{1,2,0:T(8,128)(2,1)S(1)} slice(bf16[1,260,1536]{1,2,0:T(8,128)(2,1)S(1)} %pad_maximum_fusion), slice={[0:1:1], [3:259:2], [0:1536:1]} | slice | bytes 786432 | tf_op jit(solution)/shard_map/slice | solution.py:48
  145.1 15.0 %slice.69 = bf16[1,128,1536]{1,2,0:T(8,128)(2,1)} slice(bf16[1,260,1536]{1,2,0:T(8,128)(2,1)S(1)} %pad_maximum_fusion), slice={[0:1:1], [4:260:2], [0:1536:1]} | slice | bytes 786432 | tf_op jit(solution)/shard_map/slice | solution.py:48
  160.1 1.3 rev.7
  161.4 9.3 %multiply_reduce_fusion = (f32[128,8]{0,1:T(8,128)S(1)}, f32[128,8,4096]{2,0,1:T(8,128)}) fusion(bf16[1,4096,128]{2,1,0:T(8,128)(2,1)} %all-gather.3.cloned.1.call-done, bf16[128,8,128]{2,1,0:T(8,128)(2,1)S(1)} %bitcast.92), kind=kOutput, calls=%fused_computation.1 | convolution fusion | flops 1082129408 | bytes 18092032 | tf_op jit(solution)/shard_map/qhd,kd->qhk/dot_general | solution.py:37
  170.7 8.7 %fusion = f32[128,8]{0,1:T(8,128)S(1)} fusion(f32[128,8,4096]{2,0,1:T(8,128)} %get-tuple-element.52, f32[128,8]{0,1:T(8,128)S(1)} %broadcast_maximum_fusion), kind=kLoop, calls=%fused_computation.2 | loop fusion | flops 12581888 | bytes 16785408 | tf_op jit(solution)/shard_map/reduce_sum | solution.py:42
  179.4 28.2 %all-gather.5.cloned.1.call-done = bf16[1,4096,192]{1,2,0:T(8,128)(2,1)} async-done(((bf16[1,128,192]{1,2,0:T(8,128)(2,1)}), bf16[1,4096,192]{1,2,0:T(8,128)(2,1)}) %all-gather.5.cloned.1.call-update) | async-done | bytes 1572880 | tf_op jit(solution)/shard_map/all_gather | solution.py:36
  207.6 8.0 %fusion.7 = f32[128,8,192]{0,2,1:T(8,128)S(1)} fusion(bf16[1,4096,192]{1,2,0:T(8,128)(2,1)} %all-gather.5.cloned.1.call-done, f32[128,8,4096]{2,0,1:T(8,128)} %get-tuple-element.52, f32[128,8]{0,1:T(8,128)S(1)} %broadcast_maximum_fusion, f32[128,8]{0,1:T(8,128)S(1)} %fusion), kind=kOutput, calls=%fused_computation.19 | convolution fusion | flops 1623392256 | bytes 19144704 | tf_op jit(solution)/shard_map/qhk,kv->qhv/dot_general | solution.py:43
  215.6 2.7 fusion.22
  218.5 93.2 %psum.7 = f32[5,1536]{1,0:T(8,128)S(1)} all-reduce(f32[5,1536]{1,0:T(8,128)S(1)} %stack.170), channel_id=1, replica_groups=mesh['dp'=16,'ctx'=32] {'dp','ctx'}, use_global_device_ids=true, to_apply=%region_7.0 | all-reduce | flops 7680 | bytes 61440 | tf_op jit(solution)/shard_map/psum | solution.py:72
  311.9 6.2 %collective-permute-start.2 = (bf16[1,1,1536]{1,2,0:T(8,128)(2,1)S(1)}, bf16[1,1,1536]{1,2,0:T(8,128)(2,1)S(1)}, u32[]{:S(2)}, u32[]{:S(2)}) collective-permute-start(bf16[1,1,1536]{1,2,0:T(8,128)(2,1)S(1)} %get-tuple-element.17), channel_id=1, source_target_pairs={{0,1},{1,2},{2,3},{3,4},{4,5},{5,6},{6,7},{7,8},{8,9},{9,10},{10,1... | collective-permute-start | bytes 9224 | tf_op jit(solution)/shard_map/ppermute | solution.py:19
  318.1 1.9 collective-permute-start.3
  320.0 0.6 broadcast_multiply_fusion
  320.6 11.6 %collective-permute-done.2 = bf16[1,1,1536]{1,2,0:T(8,128)(2,1)S(1)} collective-permute-done((bf16[1,1,1536]{1,2,0:T(8,128)(2,1)S(1)}, bf16[1,1,1536]{1,2,0:T(8,128)(2,1)S(1)}, u32[]{:S(2)}, u32[]{:S(2)}) %collective-permute-start.2) | collective-permute-done | bytes 3104 | tf_op jit(solution)/shard_map/ppermute | solution.py:19
  332.2 10.3 %collective-permute-done.3 = bf16[1,1,1536]{1,2,0:T(8,128)(2,1)S(1)} collective-permute-done((bf16[1,1,1536]{1,2,0:T(8,128)(2,1)S(1)}, bf16[1,1,1536]{1,2,0:T(8,128)(2,1)S(1)}, u32[]{:S(2)}, u32[]{:S(2)}) %collective-permute-start.3) | collective-permute-done | bytes 3104 | tf_op jit(solution)/shard_map/ppermute | solution.py:21
  342.9 1.7 fusion.26
  344.7 0.8 copy.123
  345.5 1.2 convert_element_type.56
  (77 shorter events, 14.4 us)
Async XLA Ops:
  7.2 154.2 %all-gather.3.cloned.1.call-start = ((), (), s32[]{:S(2)}) async-start(), calls=%async_computation.2 | async-start | bytes 1081344 | tf_op jit(solution)/shard_map/all_gather | solution.py:35
  10.8 58.8 %copy-start.1 = (bf16[1,256,1536]{2,1,0:T(8,128)(2,1)S(1)}, bf16[1,256,1536]{2,1,0:T(8,128)(2,1)}, u32[]{:S(2)}) copy-start(bf16[1,256,1536]{2,1,0:T(8,128)(2,1)} %param.9) | copy-start | bytes 2359300
  13.0 64.7 %copy-start.3 = (f32[5,1536]{1,0:T(8,128)S(1)}, f32[5,1536]{1,0:T(8,128)}, u32[]{:S(2)}) copy-start(f32[5,1536]{1,0:T(8,128)} %param.11) | copy-start | bytes 92164
  33.2 45.0 %copy-start.2 = (bf16[1,128,1024]{2,1,0:T(8,128)(2,1)S(1)}, bf16[1,128,1024]{2,1,0:T(8,128)(2,1)}, u32[]{:S(2)}) copy-start(bf16[1,128,1024]{2,1,0:T(8,128)(2,1)} %param.6) | copy-start | bytes 786436
  33.2 27.3 %all-to-all-start = ((bf16[32,1,128,48]{2,3,1,0:T(8,128)(2,1)}), bf16[32,1,128,48]{2,3,1,0:T(8,128)(2,1)S(1)}, u32[]{:S(2)}, u32[]{:S(2)}) async-start(bf16[32,1,128,48]{2,3,1,0:T(8,128)(2,1)} %constant_dynamic-update-slice_fusion), calls=%async_computation | async-start | bytes 786432 | tf_op jit(solution)/shard_map/all_to_all | solution.py:53
  47.0 160.7 %all-gather.5.cloned.1.call-start = ((), (), s32[]{:S(2)}) async-start(), calls=%async_computation.3 | async-start | bytes 1622016 | tf_op jit(solution)/shard_map/all_gather | solution.py:36
  61.2 98.9 %all-to-all-start.1 = ((bf16[32,128,48]{1,2,0:T(8,128)(2,1)}), bf16[32,128,48]{1,2,0:T(8,128)(2,1)S(1)}, u32[]{:S(2)}, u32[]{:S(2)}) async-start(bf16[32,128,48]{1,2,0:T(8,128)(2,1)} %rev.6), calls=%async_computation.1 | async-start | bytes 786432 | tf_op jit(solution)/shard_map/all_to_all | solution.py:57
  69.9 22.7 %collective-permute-start = (bf16[1,2,1536]{1,2,0:T(8,128)(2,1)S(1)}, bf16[1,2,1536]{1,2,0:T(8,128)(2,1)}, u32[]{:S(2)}, u32[]{:S(2)}) collective-permute-start(bf16[1,2,1536]{1,2,0:T(8,128)(2,1)S(1)} %copy.86), channel_id=1, source_target_pairs={{0,1},{1,2},{2,3},{3,4},{4,5},{5,6},{6,7},{7,8},{8,9},{9,10},{10,1... | collective-permute-start | bytes 18440 | tf_op jit(solution)/shard_map/ppermute | solution.py:19
  75.6 24.1 %collective-permute-start.1 = (bf16[1,2,1536]{1,2,0:T(8,128)(2,1)S(1)}, bf16[1,2,1536]{1,2,0:T(8,128)(2,1)}, u32[]{:S(2)}, u32[]{:S(2)}) collective-permute-start(bf16[1,2,1536]{1,2,0:T(8,128)(2,1)S(1)} %copy.87), channel_id=1, source_target_pairs={{1,0},{2,1},{3,2},{4,3},{5,4},{6,5},{7,6},{8,7},{9,8},{10,9},{11,1... | collective-permute-start | bytes 18440 | tf_op jit(solution)/shard_map/ppermute | solution.py:21
  179.4 36.2 %copy-start = (bf16[1,128,1536]{1,2,0:T(8,128)(2,1)S(1)}, bf16[1,128,1536]{1,2,0:T(8,128)(2,1)}, u32[]{:S(2)}) copy-start(bf16[1,128,1536]{1,2,0:T(8,128)(2,1)} %slice.69) | copy-start | bytes 1179652
  311.9 20.3 %collective-permute-start.2 = (bf16[1,1,1536]{1,2,0:T(8,128)(2,1)S(1)}, bf16[1,1,1536]{1,2,0:T(8,128)(2,1)S(1)}, u32[]{:S(2)}, u32[]{:S(2)}) collective-permute-start(bf16[1,1,1536]{1,2,0:T(8,128)(2,1)S(1)} %get-tuple-element.17), channel_id=1, source_target_pairs={{0,1},{1,2},{2,3},{3,4},{4,5},{5,6},{6,7},{7,8},{8,9},{9,10},{10,1... | collective-permute-start | bytes 9224 | tf_op jit(solution)/shard_map/ppermute | solution.py:19
  318.1 24.4 %collective-permute-start.3 = (bf16[1,1,1536]{1,2,0:T(8,128)(2,1)S(1)}, bf16[1,1,1536]{1,2,0:T(8,128)(2,1)S(1)}, u32[]{:S(2)}, u32[]{:S(2)}) collective-permute-start(bf16[1,1,1536]{1,2,0:T(8,128)(2,1)S(1)} %get-tuple-element.18), channel_id=1, source_target_pairs={{1,0},{2,1},{3,2},{4,3},{5,4},{6,5},{7,6},{8,7},{9,8},{10,9},{11,1... | collective-permute-start | bytes 9224 | tf_op jit(solution)/shard_map/ppermute | solution.py:21
Sparse Core Ops, SparseCore 0:
  11.2 110.4 all-gather.2
  124.7 82.8 all-gather.4
